TPU v7x, 32 devices: a whole 2x2x4 slice. The times are simulated.
32 devices in a mesh: groups: 2 (over x), rows: 16 (over z, y, core).
Axes of the slice: x: 2, y: 2, z: 4, core: 2. Of those that a mesh axis runs over, the one named last changes fastest.
Arguments:
- pair: bfloat16 [512, 256, 128], P(('groups', 'rows')), parts along dimension 0, may hold values from -6 to 6
- proj_weights: bfloat16 [6, 128, 128], replicated, may hold values from -0.5 to 0.5
- cotangent: bfloat16 [512, 256, 128], P(('groups', 'rows')), parts along dimension 0, may hold values from -8.5 to 8.5
Outputs:
- update: bfloat16 [512, 256, 128], P(('groups', 'rows')), parts along dimension 0
- pair_grad: bfloat16 [512, 256, 128], P(('groups', 'rows')), parts along dimension 0
- weight_grads: float32 [12, 128, 128], P('groups'), parts along dimension 0
There are 2 independent parts, one for each index of `groups`. A program takes and returns all parts, laid end to end along the dimension named above; an argument that names none is the same for every part. Nothing has to cross between parts.
All inputs are finite; a program needn't handle non-finite values.
Results may differ from a plain program's by a relative error of at most 0.015.
Values may be sent and summed in bfloat16 or wider, within the bound.
A program may use at most 128 MiB of HBM per device.

v0:
```python
import jax
import jax.numpy as jnp
from jax import lax
from jax.sharding import PartitionSpec as P


def layer_norm(values, along_dim):
    centred = values - jnp.mean(values, axis=along_dim, keepdims=True)
    inv_scale = lax.rsqrt(jnp.mean(centred * centred, axis=along_dim, keepdims=True) + 1e-05)
    return (centred * inv_scale, inv_scale)


def norm_backward(normed, inv_scale, upstream, along_dim):
    return (
        upstream
        - jnp.mean(upstream, axis=along_dim, keepdims=True)
        - normed * jnp.mean(upstream * normed, axis=along_dim, keepdims=True)
    ) * inv_scale


def triangle_slab(pieces):
    left_slab, right_slab = pieces
    product = lax.dot_general(
        left_slab, right_slab, (((3,), (3,)), ((0, 1), (0, 1))), preferred_element_type=jnp.float32
    )
    return (product.astype(jnp.bfloat16), left_slab, right_slab)


def edge_backward(upstream, left_slab, right_slab):
    left_part = lax.dot_general(
        upstream, right_slab, (((3,), (2,)), ((0, 1), (0, 1))), preferred_element_type=jnp.float32
    )
    right_part = lax.dot_general(
        upstream, left_slab, (((2,), (2,)), ((0, 1), (0, 1))), preferred_element_type=jnp.float32
    )
    return (left_part.astype(jnp.bfloat16), right_part.astype(jnp.bfloat16))


def body(pair, proj_weights, cotangent):
    residues = pair.shape[1]
    local_rows = pair.shape[0]
    chans = pair.shape[2]
    ranks = lax.axis_size("rows")
    slab_width = chans // ranks
    normed_in, scale_in = layer_norm(pair.astype(jnp.float32), 2)
    normed_bf = normed_in.astype(jnp.bfloat16)
    edge_pre = jnp.einsum(
        "ikd,ndc->ncik", normed_bf, proj_weights[0:4], preferred_element_type=jnp.float32
    )
    gate_pre = jnp.einsum(
        "ikd,dc->ikc", normed_bf, proj_weights[4], preferred_element_type=jnp.float32
    )
    left_sig = jax.nn.sigmoid(edge_pre[1])
    right_sig = jax.nn.sigmoid(edge_pre[3])
    left_edge = (
        (left_sig * edge_pre[0])
        .astype(jnp.bfloat16)
        .reshape(ranks, slab_width, local_rows, residues)
    )
    right_edge = (
        (right_sig * edge_pre[2])
        .astype(jnp.bfloat16)
        .reshape(ranks, slab_width, local_rows, residues)
    )
    products, left_held, right_held = triangle_slab(
        (
            lax.all_to_all(left_edge, "rows", split_axis=0, concat_axis=2, tiled=True),
            lax.all_to_all(right_edge, "rows", split_axis=0, concat_axis=2, tiled=True),
        )
    )
    regrouped = lax.all_to_all(products, "rows", split_axis=2, concat_axis=0, tiled=True).reshape(
        chans, local_rows, residues
    )
    normed_mid, scale_mid = layer_norm(regrouped.astype(jnp.float32), 0)
    mid_bf = normed_mid.astype(jnp.bfloat16)
    projected = jnp.einsum(
        "cij,cd->ijd", mid_bf, proj_weights[5], preferred_element_type=jnp.float32
    )
    gating = jax.nn.sigmoid(gate_pre)
    update = (gating * projected).astype(jnp.bfloat16)
    upstream = cotangent.astype(jnp.float32)
    gated_up = (upstream * gating).astype(jnp.bfloat16)
    gate_grad = (upstream * projected * gating * (1.0 - gating)).astype(jnp.bfloat16)
    out_weights = jnp.stack(
        [
            jnp.einsum("ikd,ikc->dc", normed_bf, gate_grad, preferred_element_type=jnp.float32),
            jnp.einsum("cij,ijd->cd", mid_bf, gated_up, preferred_element_type=jnp.float32),
        ]
    )
    mid_grad = jnp.einsum(
        "ijd,cd->cij", gated_up, proj_weights[5], preferred_element_type=jnp.float32
    )
    prod_grad = norm_backward(normed_mid, scale_mid, mid_grad, 0).astype(jnp.bfloat16)
    prod_grad = prod_grad.reshape(ranks, slab_width, local_rows, residues)
    slab_grad = lax.all_to_all(prod_grad, "rows", split_axis=0, concat_axis=2, tiled=True)
    left_part, right_part = edge_backward(slab_grad, left_held, right_held)
    left_back, right_back = (
        lax.all_to_all(left_part, "rows", split_axis=2, concat_axis=0, tiled=True),
        lax.all_to_all(right_part, "rows", split_axis=2, concat_axis=0, tiled=True),
    )
    left_full = left_back.reshape(chans, local_rows, residues).astype(jnp.float32)
    right_full = right_back.reshape(chans, local_rows, residues).astype(jnp.float32)
    edge_grad = jnp.stack(
        [
            left_full * left_sig,
            left_full * edge_pre[0] * left_sig * (1.0 - left_sig),
            right_full * right_sig,
            right_full * edge_pre[2] * right_sig * (1.0 - right_sig),
        ]
    ).astype(jnp.bfloat16)
    in_weights = jnp.einsum(
        "ikd,ncik->ndc", normed_bf, edge_grad, preferred_element_type=jnp.float32
    )
    input_grad = jnp.einsum(
        "ncik,ndc->ikd", edge_grad, proj_weights[0:4], preferred_element_type=jnp.float32
    )
    input_grad = input_grad + jnp.einsum(
        "ikc,dc->ikd", gate_grad, proj_weights[4], preferred_element_type=jnp.float32
    )
    pair_grad = norm_backward(normed_in, scale_in, input_grad, 2).astype(jnp.bfloat16)
    totals = lax.psum(
        jnp.concatenate([in_weights, out_weights], axis=0).astype(jnp.bfloat16), "rows"
    ).astype(jnp.float32)
    weight_grads = totals / residues
    return (update, pair_grad, weight_grads)


def solution(mesh):
    in_specs = (P(("groups", "rows"), None, None), P(), P(("groups", "rows"), None, None))
    out_specs = (
        P(("groups", "rows"), None, None),
        P(("groups", "rows"), None, None),
        P("groups", None, None),
    )
    return jax.shard_map(body, mesh=mesh, in_specs=in_specs, out_specs=out_specs, check_vma=False)
```

profile of v0, /device:TPU:0, one launch (start us, length us, event | category | flops | bytes accessed | tf_op | source)
XLA Modules:
  0.0 318.2 jit_solution(738744233146156121)
XLA Ops:
  7.2 0.0 copy-start.9
  7.2 1.5 copy.69
  8.7 0.2 convert_reduce_fusion
  8.9 0.3 fusion.9
  9.2 0.0 copy-done.9
  9.2 1.3 convolution_bitcast_fusion
  10.5 0.0 copy-start
  10.5 1.2 fusion.46
  11.7 2.0 copy-done
  13.7 1.1 copy.75
  14.8 7.4 %all-to-all-start.1 = ((bf16[16,8,16,256]{3,1,2,0:T(8,128)(2,1)}), bf16[16,8,16,256]{3,1,2,0:T(8,128)(2,1)S(1)}, u32[]{:S(2)}, u32[]{:S(2)}) async-start(bf16[16,8,16,256]{3,1,2,0:T(8,128)(2,1)} %copy.75), calls=%async_computation.1 | async-start | bytes 2097152 | tf_op jit(solution)/shard_map/all_to_all | solution.py:68
  22.2 1.1 copy.73
  23.3 21.9 %all-to-all-done.1 = bf16[16,8,16,256]{3,1,2,0:T(8,128)(2,1)S(1)} async-done(((bf16[16,8,16,256]{3,1,2,0:T(8,128)(2,1)}), bf16[16,8,16,256]{3,1,2,0:T(8,128)(2,1)S(1)}, u32[]{:S(2)}, u32[]{:S(2)}) %all-to-all-start.1) | async-done | bytes 1048608 | tf_op jit(solution)/shard_map/all_to_all | solution.py:68
  45.2 6.9 %all-to-all-start = ((bf16[16,8,16,256]{3,1,2,0:T(8,128)(2,1)}), bf16[16,8,16,256]{3,1,2,0:T(8,128)(2,1)}, u32[]{:S(2)}, u32[]{:S(2)}) async-start(bf16[16,8,16,256]{3,1,2,0:T(8,128)(2,1)} %copy.73), calls=%async_computation | async-start | bytes 2097152 | tf_op jit(solution)/shard_map/all_to_all | solution.py:67
  52.1 0.2 copy.76
  52.3 0.0 copy-start.2
  52.3 22.8 %all-to-all-done = bf16[16,8,16,256]{3,1,2,0:T(8,128)(2,1)} async-done(((bf16[16,8,16,256]{3,1,2,0:T(8,128)(2,1)}), bf16[16,8,16,256]{3,1,2,0:T(8,128)(2,1)}, u32[]{:S(2)}, u32[]{:S(2)}) %all-to-all-start) | async-done | bytes 1048608 | tf_op jit(solution)/shard_map/all_to_all | solution.py:67
  75.1 1.4 copy.74
  76.5 0.0 copy-start.1
  76.5 0.5 fusion.34
  77.0 0.0 copy-done.2
  77.0 0.6 copy.77
  77.6 0.0 copy-done.1
  77.6 31.5 %all_to_all.72 = bf16[1,8,256,256]{3,1,0,2:T(8,128)(2,1)S(1)} all-to-all(bf16[1,8,256,256]{3,1,0,2:T(8,128)(2,1)S(1)} %copy.77), channel_id=1, replica_groups=mesh['groups'=2,'rows'=16] {'rows'}, dimensions={2} | all-to-all | bytes 2097152 | tf_op jit(solution)/shard_map/all_to_all | solution.py:71
  109.1 0.3 convert_bitcast_fusion
  109.4 0.2 fusion.33
  109.6 0.3 multiply_reduce_fusion
  110.0 0.3 multiply_convert_fusion.3
  110.3 0.1 copy.79
  110.4 0.0 copy-start.7
  110.4 0.6 fusion.51
  110.9 0.7 copy-done.7
  111.6 2.5 fusion.13
  114.1 1.6 bitcast_reduce_fusion
  115.7 0.0 copy-done.5
  115.8 1.6 fusion.47
  117.4 0.1 copy.82
  117.5 29.8 %all_to_all.73 = bf16[16,8,16,256]{3,1,2,0:T(8,128)(2,1)S(1)} all-to-all(bf16[16,8,16,256]{3,1,2,0:T(8,128)(2,1)S(1)} %copy.82), channel_id=1, replica_groups=mesh['groups'=2,'rows'=16] {'rows'}, dimensions={0} | all-to-all | bytes 2097152 | tf_op jit(solution)/shard_map/all_to_all | solution.py:95
  147.3 1.0 copy-done.4
  148.3 0.2 copy.83
  148.6 0.4 fusion.35
  149.0 1.6 copy.84
  150.6 5.0 %all-to-all-start.4 = ((bf16[1,8,256,256]{3,1,0,2:T(8,128)(2,1)}), bf16[1,8,256,256]{3,1,0,2:T(8,128)(2,1)}, u32[]{:S(2)}, u32[]{:S(2)}) async-start(bf16[1,8,256,256]{3,1,0,2:T(8,128)(2,1)} %copy.84), calls=%async_computation.4 | async-start | bytes 2097152 | tf_op jit(solution)/shard_map/all_to_all | solution.py:98
  155.6 2.0 fusion.36
  157.7 1.6 copy.87
  159.3 19.3 %all-to-all-done.4 = bf16[1,8,256,256]{3,1,0,2:T(8,128)(2,1)} async-done(((bf16[1,8,256,256]{3,1,0,2:T(8,128)(2,1)}), bf16[1,8,256,256]{3,1,0,2:T(8,128)(2,1)}, u32[]{:S(2)}, u32[]{:S(2)}) %all-to-all-start.4) | async-done | bytes 1048608 | tf_op jit(solution)/shard_map/all_to_all | solution.py:98
  178.6 6.9 %all-to-all-start.5 = ((bf16[1,8,256,256]{3,1,0,2:T(8,128)(2,1)}), bf16[1,8,256,256]{3,1,0,2:T(8,128)(2,1)}, u32[]{:S(2)}, u32[]{:S(2)}) async-start(bf16[1,8,256,256]{3,1,0,2:T(8,128)(2,1)} %copy.87), calls=%async_computation.5 | async-start | bytes 2097152 | tf_op jit(solution)/shard_map/all_to_all | solution.py:99
  185.5 0.3 all-reduce.2.cloned.1.call-start
  185.8 2.0 fusion.43
  187.8 2.9 fusion.42
  190.7 17.8 %all-to-all-done.5 = bf16[1,8,256,256]{3,1,0,2:T(8,128)(2,1)} async-done(((bf16[1,8,256,256]{3,1,0,2:T(8,128)(2,1)}), bf16[1,8,256,256]{3,1,0,2:T(8,128)(2,1)}, u32[]{:S(2)}, u32[]{:S(2)}) %all-to-all-start.5) | async-done | bytes 1048608 | tf_op jit(solution)/shard_map/all_to_all | solution.py:99
  208.5 5.0 %fusion.24 = (bf16[1,128,16,256]{3,1,0,2:T(8,128)(2,1)S(1)}, bf16[1,128,16,256]{3,1,0,2:T(8,128)(2,1)S(1)}, bf16[1,128,16,256]{3,1,0,2:T(8,128)(2,1)S(1)}, bf16[1,128,16,256]{3,1,0,2:T(8,128)(2,1)S(1)}) fusion(f32[4,128,16,256]{3,1,0,2:T(8,128)} %copy-done, bf16[1,8,16,16,256]{4,1,3,2,0:T(8,128)(2,1)} %bitcast.53, bf16[1,8,16,16,256]{4,1,3,2,0:T(8,128)(2,1)} %bitcast.51), kind=kLoop, calls=%fused_computation.37 | loop fusion | flops 11534336 | bytes 14680064 | tf_op jit(solution)/shard_map/convert.17
  213.5 1.3 fusion.39
  214.8 0.0 copy-start.8
  214.8 0.7 fusion.55
  215.5 0.5 copy-done.8
  216.0 0.7 fusion.77
  216.7 0.7 pad_maximum_fusion.3
  217.5 0.0 all-reduce.2.cloned.1.call-update
  217.5 1.6 fusion.8
  219.1 2.3 copy.93
  221.3 88.2 %all-reduce.2.cloned.1.call-done = bf16[6,128,128]{1,2,0:T(8,128)(2,1)} async-done(((bf16[6,128,128]{1,2,0:T(8,128)(2,1)}), bf16[6,128,128]{1,2,0:T(8,128)(2,1)}) %all-reduce.2.cloned.1.call-update) | async-done | bytes 196624 | tf_op jit(solution)/shard_map/psum | solution.py:121
  309.5 1.0 convert_multiply_fusion.2
  310.5 0.9 copy.94
  (13 shorter events, 0.1 us)
Async XLA Ops:
  7.2 2.1 copy-start.9
  10.5 3.2 %copy-start = (f32[4,128,16,256]{3,1,0,2:T(8,128)}, f32[4,128,16,256]{3,1,0,2:T(8,128)S(1)}, u32[]{:S(2)}) copy-start(f32[4,128,16,256]{3,1,0,2:T(8,128)S(1)} %convolution_bitcast_fusion) | copy-start | bytes 25165828
  14.8 30.3 %all-to-all-start.1 = ((bf16[16,8,16,256]{3,1,2,0:T(8,128)(2,1)}), bf16[16,8,16,256]{3,1,2,0:T(8,128)(2,1)S(1)}, u32[]{:S(2)}, u32[]{:S(2)}) async-start(bf16[16,8,16,256]{3,1,2,0:T(8,128)(2,1)} %copy.75), calls=%async_computation.1 | async-start | bytes 2097152 | tf_op jit(solution)/shard_map/all_to_all | solution.py:68
  45.2 29.9 %all-to-all-start = ((bf16[16,8,16,256]{3,1,2,0:T(8,128)(2,1)}), bf16[16,8,16,256]{3,1,2,0:T(8,128)(2,1)}, u32[]{:S(2)}, u32[]{:S(2)}) async-start(bf16[16,8,16,256]{3,1,2,0:T(8,128)(2,1)} %copy.73), calls=%async_computation | async-start | bytes 2097152 | tf_op jit(solution)/shard_map/all_to_all | solution.py:67
  52.3 24.7 %copy-start.2 = (bf16[1,8,16,16,256]{4,3,2,1,0:T(8,128)(2,1)}, bf16[1,8,16,16,256]{4,3,2,1,0:T(8,128)(2,1)S(1)}, u32[]{:S(2)}) copy-start(bf16[1,8,16,16,256]{4,3,2,1,0:T(8,128)(2,1)S(1)} %copy.76) | copy-start | bytes 3145732
  76.5 1.1 copy-start.1
  110.4 1.2 copy-start.7
  114.1 1.6 copy-start.5
  117.5 31.0 %copy-start.3 = (bf16[1,8,16,16,256]{4,3,2,1,0:T(8,128)(2,1)S(1)}, bf16[1,8,16,16,256]{4,3,2,1,0:T(8,128)(2,1)}, u32[]{:S(2)}) copy-start(bf16[1,8,16,16,256]{4,3,2,1,0:T(8,128)(2,1)} %copy-done.2) | copy-start | bytes 3145732
  147.3 1.0 copy-start.4
  150.6 28.0 %all-to-all-start.4 = ((bf16[1,8,256,256]{3,1,0,2:T(8,128)(2,1)}), bf16[1,8,256,256]{3,1,0,2:T(8,128)(2,1)}, u32[]{:S(2)}, u32[]{:S(2)}) async-start(bf16[1,8,256,256]{3,1,0,2:T(8,128)(2,1)} %copy.84), calls=%async_computation.4 | async-start | bytes 2097152 | tf_op jit(solution)/shard_map/all_to_all | solution.py:98
  178.6 29.9 %all-to-all-start.5 = ((bf16[1,8,256,256]{3,1,0,2:T(8,128)(2,1)}), bf16[1,8,256,256]{3,1,0,2:T(8,128)(2,1)}, u32[]{:S(2)}, u32[]{:S(2)}) async-start(bf16[1,8,256,256]{3,1,0,2:T(8,128)(2,1)} %copy.87), calls=%async_computation.5 | async-start | bytes 2097152 | tf_op jit(solution)/shard_map/all_to_all | solution.py:99
  185.5 124.0 %all-reduce.2.cloned.1.call-start = ((), (), s32[]{:S(2)}) async-start(), calls=%async_computation.6 | async-start | bytes 393216 | tf_op jit(solution)/shard_map/psum | solution.py:121
  185.8 2.0 copy-start.6
  214.8 1.2 copy-start.8
Sparse Core Ops, SparseCore 0:
  217.6 91.8 all-reduce.1
where the time goes:
time: 319 us; the launch traced here: 318 us
  waiting for transfers between devices  170 us (53%)
  blocking collectives  61.3 us (19%)
  starting transfers between devices  26.5 us (8%)
  local copies, waits for them, and re-layouts  16.9 us (5%)
  matrix products  16.5 us (5%)
  between operations  14.4 us (5%)
  other arithmetic  12.6 us (4%)
    psum x1, waiting for transfers between devices, body(): lax.psum(jnp.concatenate([in_weights, out_weights], axis=0).astype(jnp.bf...  88.2 us
    all_to_all x1, blocking collectives, body(): lax.all_to_all(products, 'rows', split_axis=2, concat_axis=0, tiled=True)  31.5 us
    all_to_all x1, blocking collectives, body(): lax.all_to_all(prod_grad, 'rows', split_axis=0, concat_axis=2, tiled=True)  29.8 us
    all_to_all x1, waiting for transfers between devices, body(): lax.all_to_all(left_edge, 'rows', split_axis=0, concat_axis=2, tiled=True)  22.8 us
    all_to_all x1, waiting for transfers between devices, body(): lax.all_to_all(right_edge, 'rows', split_axis=0, concat_axis=2, tiled=True)  21.9 us
    all_to_all x1, waiting for transfers between devices, body(): lax.all_to_all(left_part, 'rows', split_axis=2, concat_axis=0, tiled=True)  19.3 us
    all_to_all x1, waiting for transfers between devices, body(): lax.all_to_all(right_part, 'rows', split_axis=2, concat_axis=0, tiled=True)  17.8 us
    unnamed x23, local copies, waits for them, and re-layouts  8.91 us
  transfers between devices with their start and end apart: 5, of which 5 were waited for; matrix products, arithmetic and copies ran while one was open for 4% of the time, Pallas kernels for 0%

commit v1 on v0

--- a/solution.py
+++ b/solution.py
@@ -2,6 +2,29 @@
 import jax.numpy as jnp
 from jax import lax
 from jax.sharding import PartitionSpec as P
+
+
+def in_blocks(value, dim, size):
+    lengths = value.shape
+    blocks = value.reshape(*lengths[:dim], size, lengths[dim] // size, *lengths[dim + 1 :])
+    return jnp.moveaxis(blocks, dim, 0)
+
+
+def in_order(parts, dim):
+    parts = jnp.moveaxis(parts, 0, dim)
+    lengths = parts.shape
+    return parts.reshape(*lengths[:dim], lengths[dim] * lengths[dim + 1], *lengths[dim + 2 :])
+
+
+def rotated_exchange(x, axis, split_dim, concat_dim):
+    peers, position = (lax.axis_size(axis), lax.axis_index(axis))
+    blocks = in_blocks(x, split_dim, peers)
+    outs = [blocks[position]]
+    for turn in range(1, peers):
+        sent = blocks[(position + turn) % peers]
+        outs.append(lax.ppermute(sent, axis, [(i, (i + turn) % peers) for i in range(peers)]))
+    blocks = jnp.stack(outs)[(position - jnp.arange(peers)) % peers]
+    return in_order(blocks, concat_dim)
 
 
 def layer_norm(values, along_dim):
@@ -95,7 +118,7 @@
     slab_grad = lax.all_to_all(prod_grad, "rows", split_axis=0, concat_axis=2, tiled=True)
     left_part, right_part = edge_backward(slab_grad, left_held, right_held)
     left_back, right_back = (
-        lax.all_to_all(left_part, "rows", split_axis=2, concat_axis=0, tiled=True),
+        rotated_exchange(left_part, "rows", 2, 0),
         lax.all_to_all(right_part, "rows", split_axis=2, concat_axis=0, tiled=True),
     )
     left_full = left_back.reshape(chans, local_rows, residues).astype(jnp.float32)

time: 319 us -> 353 us (1.11)
  waiting for transfers between devices: 170 us -> 220 us
  blocking collectives: 61.3 us -> 31.5 us
  starting transfers between devices: 26.5 us -> 36.5 us
    ppermute x0 -> x15, waiting for transfers between devices: none -> 68.2 us  [rotated_exchange(): lax.ppermute(sent, axis, [(i, (i + turn) % peers) for i in range(peers)])]
    all_to_all x1 -> x0, blocking collectives: 29.8 us -> none  [body(): lax.all_to_all(prod_grad, 'rows', split_axis=0, concat_axis=2, tiled=True)]
    all_to_all x1, waiting for transfers between devices: 17.8 us -> 0.01 us  [body(): lax.all_to_all(right_part, 'rows', split_axis=2, concat_axis=0, tiled=True)]
    ppermute x0 -> x15, starting transfers between devices: none -> 10.2 us  [rotated_exchange(): lax.ppermute(sent, axis, [(i, (i + turn) % peers) for i in range(peers)])]
    unnamed x23 -> x36, local copies, waits for them, and re-layouts: 8.91 us -> 8.01 us
  transfers between devices with their start and end apart: 5 -> 20, of which waited for: 5 -> 15; matrix products, arithmetic and copies ran while one was open for 4% -> 4% of each run, Pallas kernels for 0% -> 0%
where the time goes in v1:
time: 353 us; the launch traced here: 352 us
  waiting for transfers between devices  220 us (62%)
  starting transfers between devices  36.5 us (10%)
  blocking collectives  31.5 us (9%)
  local copies, waits for them, and re-layouts  18.4 us (5%)
  matrix products  16.5 us (5%)
  other arithmetic  14.8 us (4%)
  between operations  14.7 us (4%)
    psum x1, waiting for transfers between devices, body(): lax.psum(jnp.concatenate([in_weights, out_weights], axis=0).astype(jnp.bf...  89.2 us
    ppermute x15, waiting for transfers between devices, rotated_exchange(): lax.ppermute(sent, axis, [(i, (i + turn) % peers) for i in range(peers)])  68.2 us
    all_to_all x1, blocking collectives, body(): lax.all_to_all(products, 'rows', split_axis=2, concat_axis=0, tiled=True)  31.5 us
    all_to_all x1, waiting for transfers between devices, body(): lax.all_to_all(left_edge, 'rows', split_axis=0, concat_axis=2, tiled=True)  22.8 us
    all_to_all x1, waiting for transfers between devices, body(): lax.all_to_all(right_edge, 'rows', split_axis=0, concat_axis=2, tiled=True)  21.9 us
    all_to_all x1, waiting for transfers between devices, body(): lax.all_to_all(prod_grad, 'rows', split_axis=0, concat_axis=2, tiled=True)  17.9 us
    ppermute x15, starting transfers between devices, rotated_exchange(): lax.ppermute(sent, axis, [(i, (i + turn) % peers) for i in range(peers)])  10.2 us
    unnamed x36, local copies, waits for them, and re-layouts  8.01 us
  transfers between devices with their start and end apart: 20, of which 15 were waited for; matrix products, arithmetic and copies ran while one was open for 4% of the time, Pallas kernels for 0%

profile of v1, /device:TPU:0, one launch (start us, length us, event | category | flops | bytes accessed | tf_op | source)
XLA Modules:
  0.0 352.3 jit_solution(3924180620490038080)
XLA Ops:
  7.2 1.5 copy.67
  8.9 0.3 fusion.9
  9.2 1.3 convolution_bitcast_fusion
  10.5 1.2 fusion.45
  11.7 2.0 copy-done
  13.8 1.1 copy.73
  14.8 7.4 %all-to-all-start.1 = ((bf16[16,8,16,256]{3,1,2,0:T(8,128)(2,1)}), bf16[16,8,16,256]{3,1,2,0:T(8,128)(2,1)S(1)}, u32[]{:S(2)}, u32[]{:S(2)}) async-start(bf16[16,8,16,256]{3,1,2,0:T(8,128)(2,1)} %copy.73), calls=%async_computation.1 | async-start | bytes 2097152 | tf_op jit(solution)/shard_map/all_to_all | solution.py:91
  22.2 1.1 copy.71
  23.3 21.9 %all-to-all-done.1 = bf16[16,8,16,256]{3,1,2,0:T(8,128)(2,1)S(1)} async-done(((bf16[16,8,16,256]{3,1,2,0:T(8,128)(2,1)}), bf16[16,8,16,256]{3,1,2,0:T(8,128)(2,1)S(1)}, u32[]{:S(2)}, u32[]{:S(2)}) %all-to-all-start.1) | async-done | bytes 1048608 | tf_op jit(solution)/shard_map/all_to_all | solution.py:91
  45.2 6.9 %all-to-all-start = ((bf16[16,8,16,256]{3,1,2,0:T(8,128)(2,1)}), bf16[16,8,16,256]{3,1,2,0:T(8,128)(2,1)}, u32[]{:S(2)}, u32[]{:S(2)}) async-start(bf16[16,8,16,256]{3,1,2,0:T(8,128)(2,1)} %copy.71), calls=%async_computation | async-start | bytes 2097152 | tf_op jit(solution)/shard_map/all_to_all | solution.py:90
  52.3 22.8 %all-to-all-done = bf16[16,8,16,256]{3,1,2,0:T(8,128)(2,1)} async-done(((bf16[16,8,16,256]{3,1,2,0:T(8,128)(2,1)}), bf16[16,8,16,256]{3,1,2,0:T(8,128)(2,1)}, u32[]{:S(2)}, u32[]{:S(2)}) %all-to-all-start) | async-done | bytes 1048608 | tf_op jit(solution)/shard_map/all_to_all | solution.py:90
  75.1 1.4 copy.72
  76.5 0.5 fusion.34
  77.0 0.6 copy.75
  77.6 31.5 %all_to_all.63 = bf16[1,8,256,256]{3,1,0,2:T(8,128)(2,1)S(1)} all-to-all(bf16[1,8,256,256]{3,1,0,2:T(8,128)(2,1)S(1)} %copy.75), channel_id=1, replica_groups=mesh['groups'=2,'rows'=16] {'rows'}, dimensions={2} | all-to-all | bytes 2097152 | tf_op jit(solution)/shard_map/all_to_all | solution.py:94
  109.1 0.3 convert_bitcast_fusion
  109.6 0.3 multiply_reduce_fusion
  110.0 0.3 multiply_convert_fusion.3
  110.4 0.6 fusion.50
  111.0 0.7 copy-done.6
  111.6 2.5 fusion.13
  114.2 1.6 bitcast_reduce_fusion
  115.8 1.6 fusion.46
  117.4 1.1 copy.80
  118.5 5.0 %all-to-all-start.3 = ((bf16[16,8,16,256]{3,1,2,0:T(8,128)(2,1)}), bf16[16,8,16,256]{3,1,2,0:T(8,128)(2,1)}, u32[]{:S(2)}, u32[]{:S(2)}) async-start(bf16[16,8,16,256]{3,1,2,0:T(8,128)(2,1)} %copy.80), calls=%async_computation.3 | async-start | bytes 2097152 | tf_op jit(solution)/shard_map/all_to_all | solution.py:118
  123.8 2.0 fusion.42
  125.8 2.9 fusion.41
  128.7 17.9 %all-to-all-done.3 = bf16[16,8,16,256]{3,1,2,0:T(8,128)(2,1)} async-done(((bf16[16,8,16,256]{3,1,2,0:T(8,128)(2,1)}), bf16[16,8,16,256]{3,1,2,0:T(8,128)(2,1)}, u32[]{:S(2)}, u32[]{:S(2)}) %all-to-all-start.3) | async-done | bytes 1048608 | tf_op jit(solution)/shard_map/all_to_all | solution.py:118
  146.6 2.0 fusion.35
  148.6 1.6 copy.84
  150.3 1.4 copy.81
  151.7 0.4 convolution_convert_fusion.1
  152.2 6.9 %all-to-all-start.4 = ((bf16[1,8,256,256]{3,1,0,2:T(8,128)(2,1)}), bf16[1,8,256,256]{3,1,0,2:T(8,128)(2,1)}, u32[]{:S(2)}, u32[]{:S(2)}) async-start(bf16[1,8,256,256]{3,1,0,2:T(8,128)(2,1)} %copy.84), calls=%async_computation.4 | async-start | bytes 2097152 | tf_op jit(solution)/shard_map/all_to_all | solution.py:122
  159.3 4.4 %collective-permute-start.14 = (bf16[1,8,16,256]{3,2,1,0:T(8,128)(2,1)S(1)}, bf16[1,8,16,256]{3,2,1,0:T(8,128)(2,1)S(1)}, u32[]{:S(2)}, u32[]{:S(2)}) collective-permute-start(bf16[1,8,16,256]{3,2,1,0:T(8,128)(2,1)S(1)} %get-tuple-element.29), channel_id=1, source_target_pairs={{0,15},{1,0},{2,1},{3,2},{4,3},{5,4},{6,5},{7,6},{8,7},{9,8},{10,9... | collective-permute-start | bytes 196616 | tf_op jit(solution)/shard_map/ppermute | solution.py:25
  163.7 0.6 collective-permute-start.13
  164.3 0.6 collective-permute-start.11
  164.9 1.2 collective-permute-start
  166.1 18.1 %collective-permute-done = bf16[1,8,16,256]{3,2,1,0:T(8,128)(2,1)S(1)} collective-permute-done((bf16[1,8,16,256]{3,2,1,0:T(8,128)(2,1)S(1)}, bf16[1,8,16,256]{3,2,1,0:T(8,128)(2,1)S(1)}, u32[]{:S(2)}, u32[]{:S(2)}) %collective-permute-start) | collective-permute-done | bytes 65568 | tf_op jit(solution)/shard_map/ppermute | solution.py:25
  184.2 7.0 %collective-permute-done.1 = bf16[1,8,16,256]{3,2,1,0:T(8,128)(2,1)S(1)} collective-permute-done((bf16[1,8,16,256]{3,2,1,0:T(8,128)(2,1)S(1)}, bf16[1,8,16,256]{3,2,1,0:T(8,128)(2,1)S(1)}, u32[]{:S(2)}, u32[]{:S(2)}) %collective-permute-start.1) | collective-permute-done | bytes 65568 | tf_op jit(solution)/shard_map/ppermute | solution.py:25
  191.2 5.5 %collective-permute-done.2 = bf16[1,8,16,256]{3,2,1,0:T(8,128)(2,1)S(1)} collective-permute-done((bf16[1,8,16,256]{3,2,1,0:T(8,128)(2,1)S(1)}, bf16[1,8,16,256]{3,2,1,0:T(8,128)(2,1)S(1)}, u32[]{:S(2)}, u32[]{:S(2)}) %collective-permute-start.2) | collective-permute-done | bytes 65568 | tf_op jit(solution)/shard_map/ppermute | solution.py:25
  196.7 6.1 %collective-permute-done.3 = bf16[1,8,16,256]{3,2,1,0:T(8,128)(2,1)S(1)} collective-permute-done((bf16[1,8,16,256]{3,2,1,0:T(8,128)(2,1)S(1)}, bf16[1,8,16,256]{3,2,1,0:T(8,128)(2,1)S(1)}, u32[]{:S(2)}, u32[]{:S(2)}) %collective-permute-start.3) | collective-permute-done | bytes 65568 | tf_op jit(solution)/shard_map/ppermute | solution.py:25
  202.7 5.5 %collective-permute-done.4 = bf16[1,8,16,256]{3,2,1,0:T(8,128)(2,1)S(1)} collective-permute-done((bf16[1,8,16,256]{3,2,1,0:T(8,128)(2,1)S(1)}, bf16[1,8,16,256]{3,2,1,0:T(8,128)(2,1)S(1)}, u32[]{:S(2)}, u32[]{:S(2)}) %collective-permute-start.4) | collective-permute-done | bytes 65568 | tf_op jit(solution)/shard_map/ppermute | solution.py:25
  208.2 6.1 %collective-permute-done.5 = bf16[1,8,16,256]{3,2,1,0:T(8,128)(2,1)S(1)} collective-permute-done((bf16[1,8,16,256]{3,2,1,0:T(8,128)(2,1)S(1)}, bf16[1,8,16,256]{3,2,1,0:T(8,128)(2,1)S(1)}, u32[]{:S(2)}, u32[]{:S(2)}) %collective-permute-start.5) | collective-permute-done | bytes 65568 | tf_op jit(solution)/shard_map/ppermute | solution.py:25
  214.3 4.9 %collective-permute-done.6 = bf16[1,8,16,256]{3,2,1,0:T(8,128)(2,1)S(1)} collective-permute-done((bf16[1,8,16,256]{3,2,1,0:T(8,128)(2,1)S(1)}, bf16[1,8,16,256]{3,2,1,0:T(8,128)(2,1)S(1)}, u32[]{:S(2)}, u32[]{:S(2)}) %collective-permute-start.6) | collective-permute-done | bytes 65568 | tf_op jit(solution)/shard_map/ppermute | solution.py:25
  219.1 0.4 collective-permute-start.7
  219.6 4.7 %collective-permute-done.7 = bf16[1,8,16,256]{3,2,1,0:T(8,128)(2,1)S(1)} collective-permute-done((bf16[1,8,16,256]{3,2,1,0:T(8,128)(2,1)S(1)}, bf16[1,8,16,256]{3,2,1,0:T(8,128)(2,1)S(1)}, u32[]{:S(2)}, u32[]{:S(2)}) %collective-permute-start.7) | collective-permute-done | bytes 65568 | tf_op jit(solution)/shard_map/ppermute | solution.py:25
  224.3 4.6 %collective-permute-done.8 = bf16[1,8,16,256]{3,2,1,0:T(8,128)(2,1)S(1)} collective-permute-done((bf16[1,8,16,256]{3,2,1,0:T(8,128)(2,1)S(1)}, bf16[1,8,16,256]{3,2,1,0:T(8,128)(2,1)S(1)}, u32[]{:S(2)}, u32[]{:S(2)}) %collective-permute-start.8) | collective-permute-done | bytes 65568 | tf_op jit(solution)/shard_map/ppermute | solution.py:25
  228.9 1.8 collective-permute-start.9
  230.7 3.4 collective-permute-done.9
  234.1 1.2 collective-permute-start.10
  235.3 2.5 collective-permute-done.10
  237.9 1.6 gather_fusion
  239.4 1.5 convert_element_type.155
  241.0 5.7 %fusion.24 = (bf16[1,128,16,256]{3,1,0,2:T(8,128)(2,1)S(1)}, bf16[1,128,16,256]{3,1,0,2:T(8,128)(2,1)S(1)}, bf16[1,128,16,256]{3,1,0,2:T(8,128)(2,1)S(1)}, bf16[1,128,16,256]{3,1,0,2:T(8,128)(2,1)S(1)}) fusion(f32[16,8,16,256]{3,2,1,0:T(8,128)S(1)} %convert_element_type.155, f32[4,128,16,256]{3,1,0,2:T(8,128)} %copy-done, ...), kind=kLoop, calls=%fused_computation.38 | loop fusion | flops 11010048 | bytes 15728640 | tf_op jit(solution)/shard_map/convert.15
  246.6 1.3 fusion.38
  247.9 0.7 fusion.54
  248.6 0.5 copy-done.7
  249.1 0.7 fusion.78
  249.9 0.7 pad_maximum_fusion.3
  250.6 1.6 fusion.8
  252.2 2.3 copy.90
  254.4 89.2 %all-reduce.2.cloned.1.call-done = bf16[6,128,128]{1,2,0:T(8,128)(2,1)} async-done(((bf16[6,128,128]{1,2,0:T(8,128)(2,1)}), bf16[6,128,128]{1,2,0:T(8,128)(2,1)}) %all-reduce.2.cloned.1.call-update) | async-done | bytes 196624 | tf_op jit(solution)/shard_map/psum | solution.py:144
  343.6 1.0 convert_multiply_fusion.2
  344.6 0.9 copy.91
  (60 shorter events, 1.2 us)
Async XLA Ops:
  7.2 2.1 copy-start.8
  10.5 3.2 copy-start
  14.8 30.3 %all-to-all-start.1 = ((bf16[16,8,16,256]{3,1,2,0:T(8,128)(2,1)}), bf16[16,8,16,256]{3,1,2,0:T(8,128)(2,1)S(1)}, u32[]{:S(2)}, u32[]{:S(2)}) async-start(bf16[16,8,16,256]{3,1,2,0:T(8,128)(2,1)} %copy.73), calls=%async_computation.1 | async-start | bytes 2097152 | tf_op jit(solution)/shard_map/all_to_all | solution.py:91
  45.2 29.9 %all-to-all-start = ((bf16[16,8,16,256]{3,1,2,0:T(8,128)(2,1)}), bf16[16,8,16,256]{3,1,2,0:T(8,128)(2,1)}, u32[]{:S(2)}, u32[]{:S(2)}) async-start(bf16[16,8,16,256]{3,1,2,0:T(8,128)(2,1)} %copy.71), calls=%async_computation | async-start | bytes 2097152 | tf_op jit(solution)/shard_map/all_to_all | solution.py:90
  52.3 24.7 %copy-start.1 = (bf16[1,8,16,16,256]{4,3,2,1,0:T(8,128)(2,1)}, bf16[1,8,16,16,256]{4,3,2,1,0:T(8,128)(2,1)S(1)}, u32[]{:S(2)}) copy-start(bf16[1,8,16,16,256]{4,3,2,1,0:T(8,128)(2,1)S(1)} %copy.74) | copy-start | bytes 3145732
  76.5 1.1 copy-start.3
  110.4 1.2 copy-start.6
  114.2 1.6 copy-start.4
  118.5 28.0 %all-to-all-start.3 = ((bf16[16,8,16,256]{3,1,2,0:T(8,128)(2,1)}), bf16[16,8,16,256]{3,1,2,0:T(8,128)(2,1)}, u32[]{:S(2)}, u32[]{:S(2)}) async-start(bf16[16,8,16,256]{3,1,2,0:T(8,128)(2,1)} %copy.80), calls=%async_computation.3 | async-start | bytes 2097152 | tf_op jit(solution)/shard_map/all_to_all | solution.py:118
  123.8 2.0 copy-start.5
  148.6 3.1 copy-start.2
  152.2 88.8 %all-to-all-start.4 = ((bf16[1,8,256,256]{3,1,0,2:T(8,128)(2,1)}), bf16[1,8,256,256]{3,1,0,2:T(8,128)(2,1)}, u32[]{:S(2)}, u32[]{:S(2)}) async-start(bf16[1,8,256,256]{3,1,0,2:T(8,128)(2,1)} %copy.84), calls=%async_computation.4 | async-start | bytes 2097152 | tf_op jit(solution)/shard_map/all_to_all | solution.py:122
  159.1 184.5 %all-reduce.2.cloned.1.call-start = ((), (), s32[]{:S(2)}) async-start(), calls=%async_computation.5 | async-start | bytes 393216 | tf_op jit(solution)/shard_map/psum | solution.py:144
  159.3 78.5 %collective-permute-start.14 = (bf16[1,8,16,256]{3,2,1,0:T(8,128)(2,1)S(1)}, bf16[1,8,16,256]{3,2,1,0:T(8,128)(2,1)S(1)}, u32[]{:S(2)}, u32[]{:S(2)}) collective-permute-start(bf16[1,8,16,256]{3,2,1,0:T(8,128)(2,1)S(1)} %get-tuple-element.29), channel_id=1, source_target_pairs={{0,15},{1,0},{2,1},{3,2},{4,3},{5,4},{6,5},{7,6},{8,7},{9,8},{10,9... | collective-permute-start | bytes 196616 | tf_op jit(solution)/shard_map/ppermute | solution.py:25
  163.7 74.1 %collective-permute-start.13 = (bf16[1,8,16,256]{3,2,1,0:T(8,128)(2,1)S(1)}, bf16[1,8,16,256]{3,2,1,0:T(8,128)(2,1)S(1)}, u32[]{:S(2)}, u32[]{:S(2)}) collective-permute-start(bf16[1,8,16,256]{3,2,1,0:T(8,128)(2,1)S(1)} %get-tuple-element.30), channel_id=1, source_target_pairs={{0,14},{1,15},{2,0},{3,1},{4,2},{5,3},{6,4},{7,5},{8,6},{9,7},{10,... | collective-permute-start | bytes 196616 | tf_op jit(solution)/shard_map/ppermute | solution.py:25
  164.2 73.6 %collective-permute-start.12 = (bf16[1,8,16,256]{3,2,1,0:T(8,128)(2,1)S(1)}, bf16[1,8,16,256]{3,2,1,0:T(8,128)(2,1)S(1)}, u32[]{:S(2)}, u32[]{:S(2)}) collective-permute-start(bf16[1,8,16,256]{3,2,1,0:T(8,128)(2,1)S(1)} %get-tuple-element.31), channel_id=1, source_target_pairs={{0,13},{1,14},{2,15},{3,0},{4,1},{5,2},{6,3},{7,4},{8,5},{9,6},{10... | collective-permute-start | bytes 196616 | tf_op jit(solution)/shard_map/ppermute | solution.py:25
  164.3 73.5 %collective-permute-start.11 = (bf16[1,8,16,256]{3,2,1,0:T(8,128)(2,1)S(1)}, bf16[1,8,16,256]{3,2,1,0:T(8,128)(2,1)S(1)}, u32[]{:S(2)}, u32[]{:S(2)}) collective-permute-start(bf16[1,8,16,256]{3,2,1,0:T(8,128)(2,1)S(1)} %get-tuple-element.32), channel_id=1, source_target_pairs={{0,12},{1,13},{2,14},{3,15},{4,0},{5,1},{6,2},{7,3},{8,4},{9,5},{1... | collective-permute-start | bytes 196616 | tf_op jit(solution)/shard_map/ppermute | solution.py:25
  164.9 19.3 %collective-permute-start = (bf16[1,8,16,256]{3,2,1,0:T(8,128)(2,1)S(1)}, bf16[1,8,16,256]{3,2,1,0:T(8,128)(2,1)S(1)}, u32[]{:S(2)}, u32[]{:S(2)}) collective-permute-start(bf16[1,8,16,256]{3,2,1,0:T(8,128)(2,1)S(1)} %get-tuple-element.43), channel_id=1, source_target_pairs={{0,1},{1,2},{2,3},{3,4},{4,5},{5,6},{6,7},{7,8},{8,9},{9,10},{10,1... | collective-permute-start | bytes 196616 | tf_op jit(solution)/shard_map/ppermute | solution.py:25
  184.2 7.0 %collective-permute-start.1 = (bf16[1,8,16,256]{3,2,1,0:T(8,128)(2,1)S(1)}, bf16[1,8,16,256]{3,2,1,0:T(8,128)(2,1)S(1)}, u32[]{:S(2)}, u32[]{:S(2)}) collective-permute-start(bf16[1,8,16,256]{3,2,1,0:T(8,128)(2,1)S(1)} %get-tuple-element.42), channel_id=1, source_target_pairs={{0,2},{1,3},{2,4},{3,5},{4,6},{5,7},{6,8},{7,9},{8,10},{9,11},{10,... | collective-permute-start | bytes 196616 | tf_op jit(solution)/shard_map/ppermute | solution.py:25
  191.2 5.5 %collective-permute-start.2 = (bf16[1,8,16,256]{3,2,1,0:T(8,128)(2,1)S(1)}, bf16[1,8,16,256]{3,2,1,0:T(8,128)(2,1)S(1)}, u32[]{:S(2)}, u32[]{:S(2)}) collective-permute-start(bf16[1,8,16,256]{3,2,1,0:T(8,128)(2,1)S(1)} %get-tuple-element.41), channel_id=1, source_target_pairs={{0,3},{1,4},{2,5},{3,6},{4,7},{5,8},{6,9},{7,10},{8,11},{9,12},{10... | collective-permute-start | bytes 196616 | tf_op jit(solution)/shard_map/ppermute | solution.py:25
  196.7 6.1 %collective-permute-start.3 = (bf16[1,8,16,256]{3,2,1,0:T(8,128)(2,1)S(1)}, bf16[1,8,16,256]{3,2,1,0:T(8,128)(2,1)S(1)}, u32[]{:S(2)}, u32[]{:S(2)}) collective-permute-start(bf16[1,8,16,256]{3,2,1,0:T(8,128)(2,1)S(1)} %get-tuple-element.40), channel_id=1, source_target_pairs={{0,4},{1,5},{2,6},{3,7},{4,8},{5,9},{6,10},{7,11},{8,12},{9,13},{1... | collective-permute-start | bytes 196616 | tf_op jit(solution)/shard_map/ppermute | solution.py:25
  202.7 5.5 %collective-permute-start.4 = (bf16[1,8,16,256]{3,2,1,0:T(8,128)(2,1)S(1)}, bf16[1,8,16,256]{3,2,1,0:T(8,128)(2,1)S(1)}, u32[]{:S(2)}, u32[]{:S(2)}) collective-permute-start(bf16[1,8,16,256]{3,2,1,0:T(8,128)(2,1)S(1)} %get-tuple-element.39), channel_id=1, source_target_pairs={{0,5},{1,6},{2,7},{3,8},{4,9},{5,10},{6,11},{7,12},{8,13},{9,14},{... | collective-permute-start | bytes 196616 | tf_op jit(solution)/shard_map/ppermute | solution.py:25
  208.2 6.1 %collective-permute-start.5 = (bf16[1,8,16,256]{3,2,1,0:T(8,128)(2,1)S(1)}, bf16[1,8,16,256]{3,2,1,0:T(8,128)(2,1)S(1)}, u32[]{:S(2)}, u32[]{:S(2)}) collective-permute-start(bf16[1,8,16,256]{3,2,1,0:T(8,128)(2,1)S(1)} %get-tuple-element.38), channel_id=1, source_target_pairs={{0,6},{1,7},{2,8},{3,9},{4,10},{5,11},{6,12},{7,13},{8,14},{9,15},... | collective-permute-start | bytes 196616 | tf_op jit(solution)/shard_map/ppermute | solution.py:25
  214.3 4.9 %collective-permute-start.6 = (bf16[1,8,16,256]{3,2,1,0:T(8,128)(2,1)S(1)}, bf16[1,8,16,256]{3,2,1,0:T(8,128)(2,1)S(1)}, u32[]{:S(2)}, u32[]{:S(2)}) collective-permute-start(bf16[1,8,16,256]{3,2,1,0:T(8,128)(2,1)S(1)} %get-tuple-element.37), channel_id=1, source_target_pairs={{0,7},{1,8},{2,9},{3,10},{4,11},{5,12},{6,13},{7,14},{8,15},{9,0},... | collective-permute-start | bytes 196616 | tf_op jit(solution)/shard_map/ppermute | solution.py:25
  219.1 5.2 %collective-permute-start.7 = (bf16[1,8,16,256]{3,2,1,0:T(8,128)(2,1)S(1)}, bf16[1,8,16,256]{3,2,1,0:T(8,128)(2,1)S(1)}, u32[]{:S(2)}, u32[]{:S(2)}) collective-permute-start(bf16[1,8,16,256]{3,2,1,0:T(8,128)(2,1)S(1)} %get-tuple-element.36), channel_id=1, source_target_pairs={{0,8},{1,9},{2,10},{3,11},{4,12},{5,13},{6,14},{7,15},{8,0},{9,1},... | collective-permute-start | bytes 196616 | tf_op jit(solution)/shard_map/ppermute | solution.py:25
  224.3 4.6 %collective-permute-start.8 = (bf16[1,8,16,256]{3,2,1,0:T(8,128)(2,1)S(1)}, bf16[1,8,16,256]{3,2,1,0:T(8,128)(2,1)S(1)}, u32[]{:S(2)}, u32[]{:S(2)}) collective-permute-start(bf16[1,8,16,256]{3,2,1,0:T(8,128)(2,1)S(1)} %get-tuple-element.35), channel_id=1, source_target_pairs={{0,9},{1,10},{2,11},{3,12},{4,13},{5,14},{6,15},{7,0},{8,1},{9,2},... | collective-permute-start | bytes 196616 | tf_op jit(solution)/shard_map/ppermute | solution.py:25
  228.9 5.2 %collective-permute-start.9 = (bf16[1,8,16,256]{3,2,1,0:T(8,128)(2,1)S(1)}, bf16[1,8,16,256]{3,2,1,0:T(8,128)(2,1)S(1)}, u32[]{:S(2)}, u32[]{:S(2)}) collective-permute-start(bf16[1,8,16,256]{3,2,1,0:T(8,128)(2,1)S(1)} %get-tuple-element.34), channel_id=1, source_target_pairs={{0,10},{1,11},{2,12},{3,13},{4,14},{5,15},{6,0},{7,1},{8,2},{9,3},... | collective-permute-start | bytes 196616 | tf_op jit(solution)/shard_map/ppermute | solution.py:25
  234.1 3.7 %collective-permute-start.10 = (bf16[1,8,16,256]{3,2,1,0:T(8,128)(2,1)S(1)}, bf16[1,8,16,256]{3,2,1,0:T(8,128)(2,1)S(1)}, u32[]{:S(2)}, u32[]{:S(2)}) collective-permute-start(bf16[1,8,16,256]{3,2,1,0:T(8,128)(2,1)S(1)} %get-tuple-element.33), channel_id=1, source_target_pairs={{0,11},{1,12},{2,13},{3,14},{4,15},{5,0},{6,1},{7,2},{8,3},{9,4},{... | collective-permute-start | bytes 196616 | tf_op jit(solution)/shard_map/ppermute | solution.py:25
  247.9 1.2 copy-start.7
Sparse Core Ops, SparseCore 0:
  250.7 92.8 all-reduce.1
